TPU v7x, 256 devices: a whole 4x4x8 slice. The times are simulated.
256 devices in a mesh: ctx: 128 (over x, z, y_hi, core), ch: 2 (over y_lo).
Axes of the slice: x: 4, y: 4 (y_hi: 2, y_lo: 2; y = y_hi * 2 + y_lo), z: 8, core: 2. Of those that a mesh axis runs over, the one named last changes fastest.
Arguments:
- queries: bfloat16 [32768, 4096], P('ctx', 'ch'), may hold values from -6 to 6
- keys: bfloat16 [32768, 4096], P('ctx', 'ch'), may hold values from -6 to 6
- values: bfloat16 [32768, 4096], P('ctx', 'ch'), may hold values from -6 to 6
- grad_out: bfloat16 [32768, 4096], P('ctx', 'ch'), may hold values from -0.0009765625 to 0.0009765625
Outputs:
- filter_grad: float32 [4, 1024], P('ch')
All inputs are finite; a program needn't handle non-finite values.
Results may differ from a plain program's by a relative error of at most 0.004.
Values may be sent and summed in bfloat16 or wider, within the bound.
No kernel may reach another device: no remote copies, remote signals or barrier semaphores. Data moves between devices by JAX's collectives and lax.ppermute only.
A program may use at most 64 MiB of HBM per device.

v0:
```python
import jax
import jax.numpy as jnp
from jax import lax
from jax.sharding import PartitionSpec as P

GROUP_CH = 1024
HOPS = 4


def from_behind(shard, axis, by):
    peers = lax.axis_size(axis)
    pairs = [(i, i + by) for i in range(peers) if 0 <= i + by < peers]
    return lax.ppermute(shard, axis, pairs)


def lag_sums(product):
    count = product.shape[0]
    tok_rows = product.shape[1]
    padded = jnp.pad(product, ((0, 0), (0, 0), (0, tok_rows)))
    flat = padded.reshape(count, tok_rows * 2 * tok_rows)[:, : tok_rows * (2 * tok_rows - 1)]
    return jnp.sum(flat.reshape(count, tok_rows, 2 * tok_rows - 1), axis=1)


def on_device(queries, keys, values, grad_out):
    mixed = (keys.astype(jnp.float32) * values.astype(jnp.float32)).astype(jnp.bfloat16)
    weighted = (queries.astype(jnp.float32) * grad_out.astype(jnp.float32)).astype(jnp.bfloat16)
    tok_rows = mixed.shape[0]
    groups_here = mixed.shape[1] // GROUP_CH
    blocks = [mixed]
    for offset in range(HOPS):
        blocks.append(from_behind(blocks[-1], "ctx", 1))
    target_rows = weighted.reshape(tok_rows, groups_here, GROUP_CH)
    totals = jnp.zeros((groups_here, (HOPS + 2) * tok_rows), jnp.float32)
    for distance in range(HOPS + 1):
        flipped = blocks[distance][::-1].reshape(tok_rows, groups_here, GROUP_CH)
        product = jnp.einsum(
            "tgc,sgc->gts", target_rows, flipped, preferred_element_type=jnp.float32
        )
        summed = lag_sums(product)
        begin = distance * tok_rows + 1
        totals = totals.at[:, begin : begin + 2 * tok_rows - 1].add(summed)
    partial_value = totals[:, tok_rows : tok_rows + HOPS * tok_rows]
    return lax.psum(partial_value, "ctx")


def solution(mesh):
    in_specs = (P("ctx", "ch"), P("ctx", "ch"), P("ctx", "ch"), P("ctx", "ch"))
    out_specs = P("ch", None)
    return jax.shard_map(
        on_device, mesh=mesh, in_specs=in_specs, out_specs=out_specs, check_vma=False
    )
```

profile of v0, /device:TPU:8, one launch (start us, length us, event | category | flops | bytes accessed | tf_op | source)
XLA Modules:
  0.0 446.7 jit_solution(9498662420436601433)
XLA Ops:
  0.0 1.9 multiply_convert_fusion
  2.0 2.9 collective-permute-start
  4.8 1.4 collective-permute-done
  6.2 14.8 %collective-permute-start.1 = (bf16[256,2048]{1,0:T(8,128)(2,1)}, bf16[256,2048]{1,0:T(8,128)(2,1)}, u32[]{:S(2)}, u32[]{:S(2)}) collective-permute-start(bf16[256,2048]{1,0:T(8,128)(2,1)} %collective-permute-done), channel_id=1, source_target_pairs={{0,2},{2,4},{4,6},{6,8},{8,10},{10,12},{12,14},{14,16},{16,18},{18... | collective-permute-start | bytes 3145736 | tf_op jit(solution)/shard_map/ppermute | solution.py:13
  21.1 10.3 %rev.15 = bf16[256,2048]{1,0:T(8,128)(2,1)} reverse(bf16[256,2048]{1,0:T(8,128)(2,1)S(1)} %multiply_convert_fusion), dimensions={0} | reverse | bytes 2097152 | tf_op jit(solution)/shard_map/rev | solution.py:35
  31.4 0.4 multiply_convert_fusion.1
  31.8 7.3 %collective-permute-start.2 = (bf16[256,2048]{1,0:T(8,128)(2,1)}, bf16[256,2048]{1,0:T(8,128)(2,1)}, u32[]{:S(2)}, u32[]{:S(2)}) collective-permute-start(bf16[256,2048]{1,0:T(8,128)(2,1)} %collective-permute-done.1), channel_id=1, source_target_pairs={{0,2},{2,4},{4,6},{6,8},{8,10},{10,12},{12,14},{14,16},{16,18},{18... | collective-permute-start | bytes 3145736 | tf_op jit(solution)/shard_map/ppermute | solution.py:13
  39.1 0.5 fusion.12
  39.5 0.1 pad_bitcast_fusion.4
  39.7 0.8 copy.31
  40.6 1.2 reshape.169
  41.8 0.1 reduce_sum.45
  41.9 0.6 compare_reduce_fusion.3
  42.5 0.6 broadcast_select_fusion
  43.3 0.6 compare_reduce_fusion.2
  43.9 0.6 compare_reduce_fusion.1
  44.6 0.7 compare_reduce_fusion
  45.2 12.7 %rev.16 = bf16[256,2048]{1,0:T(8,128)(2,1)S(1)} reverse(bf16[256,2048]{1,0:T(8,128)(2,1)} %collective-permute-done), dimensions={0} | reverse | bytes 2097152 | tf_op jit(solution)/shard_map/rev | solution.py:35
  57.9 0.5 fusion.9
  58.4 0.1 pad_bitcast_fusion.3
  58.5 0.8 copy.32
  59.4 1.2 reshape.172
  60.8 0.7 add_select_fusion.2
  61.4 0.4 scatter-add.19
  61.8 12.6 %rev.17 = bf16[256,2048]{1,0:T(8,128)(2,1)S(1)} reverse(bf16[256,2048]{1,0:T(8,128)(2,1)} %collective-permute-done.1), dimensions={0} | reverse | bytes 2097152 | tf_op jit(solution)/shard_map/rev | solution.py:35
  74.5 6.0 %collective-permute-start.3 = (bf16[256,2048]{1,0:T(8,128)(2,1)}, bf16[256,2048]{1,0:T(8,128)(2,1)}, u32[]{:S(2)}, u32[]{:S(2)}) collective-permute-start(bf16[256,2048]{1,0:T(8,128)(2,1)} %collective-permute-done.2), channel_id=1, source_target_pairs={{0,2},{2,4},{4,6},{6,8},{8,10},{10,12},{12,14},{14,16},{16,18},{18... | collective-permute-start | bytes 3145736 | tf_op jit(solution)/shard_map/ppermute | solution.py:13
  80.4 0.5 fusion.6
  80.9 0.1 pad_bitcast_fusion.2
  81.0 0.8 copy.33
  81.9 1.2 reshape.175
  83.2 0.1 reduce_sum.47
  83.2 0.7 add_select_fusion.1
  83.9 0.3 scatter-add.20
  84.3 12.6 %rev.18 = bf16[256,2048]{1,0:T(8,128)(2,1)S(1)} reverse(bf16[256,2048]{1,0:T(8,128)(2,1)} %collective-permute-done.2), dimensions={0} | reverse | bytes 2097152 | tf_op jit(solution)/shard_map/rev | solution.py:35
  96.9 0.5 fusion.3
  97.4 0.1 pad_bitcast_fusion.1
  97.5 0.8 copy.34
  98.4 1.2 reshape.178
  99.6 0.1 reduce_sum.48
  99.7 0.7 add_select_fusion
  100.4 0.3 scatter-add.21
  100.7 12.6 %rev.19 = bf16[256,2048]{1,0:T(8,128)(2,1)S(1)} reverse(bf16[256,2048]{1,0:T(8,128)(2,1)} %collective-permute-done.3), dimensions={0} | reverse | bytes 2097152 | tf_op jit(solution)/shard_map/rev | solution.py:35
  113.4 0.5 fusion
  113.8 0.1 pad_bitcast_fusion
  114.0 0.8 copy.35
  114.9 1.2 reshape.181
  116.3 0.3 scatter-add.24
  116.6 330.1 %psum.7 = f32[2,1024]{1,0:T(2,128)} all-reduce(f32[2,1024]{1,0:T(2,128)S(1)} %slice.128), channel_id=1, replica_groups=mesh['ctx'=128,'ch'=2] {'ctx'}, use_global_device_ids=true, to_apply=%region_9.10 | all-reduce | flops 2048 | bytes 16384 | tf_op jit(solution)/shard_map/psum | solution.py:43
  (23 shorter events, 0.7 us)
Async XLA Ops:
  1.9 29.4 %copy-start = (bf16[256,2048]{1,0:T(8,128)(2,1)S(1)}, bf16[256,2048]{1,0:T(8,128)(2,1)}, u32[]{:S(2)}) copy-start(bf16[256,2048]{1,0:T(8,128)(2,1)} %param.17) | copy-start | bytes 3145732
  1.9 29.4 %copy-start.1 = (bf16[256,2048]{1,0:T(8,128)(2,1)S(1)}, bf16[256,2048]{1,0:T(8,128)(2,1)}, u32[]{:S(2)}) copy-start(bf16[256,2048]{1,0:T(8,128)(2,1)} %param.14) | copy-start | bytes 3145732
  2.0 4.3 collective-permute-start
  6.2 25.5 %collective-permute-start.1 = (bf16[256,2048]{1,0:T(8,128)(2,1)}, bf16[256,2048]{1,0:T(8,128)(2,1)}, u32[]{:S(2)}, u32[]{:S(2)}) collective-permute-start(bf16[256,2048]{1,0:T(8,128)(2,1)} %collective-permute-done), channel_id=1, source_target_pairs={{0,2},{2,4},{4,6},{6,8},{8,10},{10,12},{12,14},{14,16},{16,18},{18... | collective-permute-start | bytes 3145736 | tf_op jit(solution)/shard_map/ppermute | solution.py:13
  31.4 7.7 %copy-start.4 = (bf16[256,2048]{1,0:T(8,128)(2,1)S(1)}, bf16[256,2048]{1,0:T(8,128)(2,1)}, u32[]{:S(2)}) copy-start(bf16[256,2048]{1,0:T(8,128)(2,1)} %rev.15) | copy-start | bytes 3145732
  31.8 7.3 %copy-start.2 = (bf16[256,2048]{1,0:T(8,128)(2,1)}, bf16[256,2048]{1,0:T(8,128)(2,1)S(1)}, u32[]{:S(2)}) copy-start(bf16[256,2048]{1,0:T(8,128)(2,1)S(1)} %multiply_convert_fusion.1) | copy-start | bytes 3145732
  31.8 42.7 %collective-permute-start.2 = (bf16[256,2048]{1,0:T(8,128)(2,1)}, bf16[256,2048]{1,0:T(8,128)(2,1)}, u32[]{:S(2)}, u32[]{:S(2)}) collective-permute-start(bf16[256,2048]{1,0:T(8,128)(2,1)} %collective-permute-done.1), channel_id=1, source_target_pairs={{0,2},{2,4},{4,6},{6,8},{8,10},{10,12},{12,14},{14,16},{16,18},{18... | collective-permute-start | bytes 3145736 | tf_op jit(solution)/shard_map/ppermute | solution.py:13
  45.2 12.7 %copy-start.3 = (bf16[256,2048]{1,0:T(8,128)(2,1)S(1)}, bf16[256,2048]{1,0:T(8,128)(2,1)}, u32[]{:S(2)}) copy-start(bf16[256,2048]{1,0:T(8,128)(2,1)} %copy-done.2) | copy-start | bytes 3145732
  74.5 26.3 %collective-permute-start.3 = (bf16[256,2048]{1,0:T(8,128)(2,1)}, bf16[256,2048]{1,0:T(8,128)(2,1)}, u32[]{:S(2)}, u32[]{:S(2)}) collective-permute-start(bf16[256,2048]{1,0:T(8,128)(2,1)} %collective-permute-done.2), channel_id=1, source_target_pairs={{0,2},{2,4},{4,6},{6,8},{8,10},{10,12},{12,14},{14,16},{16,18},{18... | collective-permute-start | bytes 3145736 | tf_op jit(solution)/shard_map/ppermute | solution.py:13
where the time goes:
time: 451 us; the launch traced here: 447 us
  blocking collectives  330 us (73%)
  local copies, waits for them, and re-layouts  73.4 us (16%)
  starting transfers between devices  31 us (7%)
  other arithmetic  8.06 us (2%)
    psum x1, blocking collectives, on_device(): return lax.psum(partial_value, 'ctx')  330 us
    rev x5, local copies, waits for them, and re-layouts, on_device(): flipped = blocks[distance][::-1].reshape(tok_rows, groups_here, GROUP_CH)  60.8 us
    ppermute x4, starting transfers between devices, from_behind(): return lax.ppermute(shard, axis, pairs)  31 us
  transfers between devices with their start and end apart: 4, of which 1 were waited for; matrix products, arithmetic and copies ran while one was open for 15% of the time, Pallas kernels for 0%

commit v1 on v0

--- a/solution.py
+++ b/solution.py
@@ -40,7 +40,7 @@
         begin = distance * tok_rows + 1
         totals = totals.at[:, begin : begin + 2 * tok_rows - 1].add(summed)
     partial_value = totals[:, tok_rows : tok_rows + HOPS * tok_rows]
-    return lax.psum(partial_value, "ctx")
+    return jnp.sum(lax.all_gather(partial_value, "ctx"), axis=0)
 
 
 def solution(mesh):

time: 451 us -> 246 us (0.55)
  the two profiles are of different devices: /device:TPU:8 before, /device:TPU:1 now
where the time goes in v1:
time: 246 us; the launch traced here: 242 us
  waiting for transfers between devices  121 us (49%)
  local copies, waits for them, and re-layouts  74 us (30%)
  starting transfers between devices  20.3 us (8%)
  between operations  13.8 us (6%)
  other arithmetic  10.2 us (4%)
    all_gather x1, waiting for transfers between devices, on_device(): return jnp.sum(lax.all_gather(partial_value, 'ctx'), axis=0)  108 us
    rev x5, local copies, waits for them, and re-layouts, on_device(): flipped = blocks[distance][::-1].reshape(tok_rows, groups_here, GROUP_CH)  60.8 us
    ppermute x4, starting transfers between devices, from_behind(): return lax.ppermute(shard, axis, pairs)  20.3 us
    ppermute x4, waiting for transfers between devices, from_behind(): return lax.ppermute(shard, axis, pairs)  13.1 us
    reshape x5, local copies, waits for them, and re-layouts, lag_sums(): return jnp.sum(flat.reshape(count, tok_rows, 2 * tok_rows - 1), axis=1)  6.16 us
    unnamed x21, local copies, waits for them, and re-layouts  5.29 us
    another operation x8, other arithmetic  5.26 us
  transfers between devices with their start and end apart: 5, of which 3 were waited for; matrix products, arithmetic and copies ran while one was open for 27% of the time, Pallas kernels for 0%

profile of v1, /device:TPU:1, one launch (start us, length us, event | category | flops | bytes accessed | tf_op | source)
XLA Modules:
  0.0 241.6 jit_solution(14428941229039422685)
XLA Ops:
  6.5 1.9 multiply_convert_fusion
  8.5 6.3 %collective-permute-start = (bf16[256,2048]{1,0:T(8,128)(2,1)S(1)}, bf16[256,2048]{1,0:T(8,128)(2,1)}, u32[]{:S(2)}, u32[]{:S(2)}) collective-permute-start(bf16[256,2048]{1,0:T(8,128)(2,1)S(1)} %multiply_convert_fusion), channel_id=1, source_target_pairs={{0,2},{2,4},{4,6},{6,8},{8,10},{10,12},{12,14},{14,16},{16,18},{18... | collective-permute-start | bytes 3145736 | tf_op jit(solution)/shard_map/ppermute | solution.py:13
  14.9 11.7 %collective-permute-done = bf16[256,2048]{1,0:T(8,128)(2,1)} collective-permute-done((bf16[256,2048]{1,0:T(8,128)(2,1)S(1)}, bf16[256,2048]{1,0:T(8,128)(2,1)}, u32[]{:S(2)}, u32[]{:S(2)}) %collective-permute-start) | collective-permute-done | bytes 1048608 | tf_op jit(solution)/shard_map/ppermute | solution.py:13
  26.6 6.0 %collective-permute-start.1 = (bf16[256,2048]{1,0:T(8,128)(2,1)}, bf16[256,2048]{1,0:T(8,128)(2,1)}, u32[]{:S(2)}, u32[]{:S(2)}) collective-permute-start(bf16[256,2048]{1,0:T(8,128)(2,1)} %collective-permute-done), channel_id=1, source_target_pairs={{0,2},{2,4},{4,6},{6,8},{8,10},{10,12},{12,14},{14,16},{16,18},{18... | collective-permute-start | bytes 3145736 | tf_op jit(solution)/shard_map/ppermute | solution.py:13
  32.6 10.3 %rev.15 = bf16[256,2048]{1,0:T(8,128)(2,1)} reverse(bf16[256,2048]{1,0:T(8,128)(2,1)S(1)} %multiply_convert_fusion), dimensions={0} | reverse | bytes 2097152 | tf_op jit(solution)/shard_map/rev | solution.py:35
  42.9 0.4 multiply_convert_fusion.1
  43.3 1.3 collective-permute-done.1
  44.6 5.9 %collective-permute-start.2 = (bf16[256,2048]{1,0:T(8,128)(2,1)}, bf16[256,2048]{1,0:T(8,128)(2,1)}, u32[]{:S(2)}, u32[]{:S(2)}) collective-permute-start(bf16[256,2048]{1,0:T(8,128)(2,1)} %collective-permute-done.1), channel_id=1, source_target_pairs={{0,2},{2,4},{4,6},{6,8},{8,10},{10,12},{12,14},{14,16},{16,18},{18... | collective-permute-start | bytes 3145736 | tf_op jit(solution)/shard_map/ppermute | solution.py:13
  50.5 0.5 fusion.12
  51.0 0.1 pad_bitcast_fusion.4
  51.1 0.8 copy.41
  52.0 1.2 reshape.169
  53.3 0.6 compare_reduce_fusion.3
  54.0 0.6 broadcast_select_fusion
  54.7 0.6 compare_reduce_fusion.2
  55.4 0.6 compare_reduce_fusion.1
  56.0 0.7 compare_reduce_fusion
  56.7 12.7 %rev.16 = bf16[256,2048]{1,0:T(8,128)(2,1)S(1)} reverse(bf16[256,2048]{1,0:T(8,128)(2,1)} %collective-permute-done), dimensions={0} | reverse | bytes 2097152 | tf_op jit(solution)/shard_map/rev | solution.py:35
  69.4 0.5 fusion.9
  69.9 0.1 pad_bitcast_fusion.3
  70.0 0.8 copy.42
  70.9 1.2 reshape.172
  72.2 0.7 add_select_fusion.2
  72.9 0.4 scatter-add.19
  73.3 12.6 %rev.17 = bf16[256,2048]{1,0:T(8,128)(2,1)S(1)} reverse(bf16[256,2048]{1,0:T(8,128)(2,1)} %collective-permute-done.1), dimensions={0} | reverse | bytes 2097152 | tf_op jit(solution)/shard_map/rev | solution.py:35
  85.9 2.1 collective-permute-start.3
  88.0 0.5 fusion.6
  88.5 0.1 pad_bitcast_fusion.2
  88.6 0.8 copy.43
  89.5 1.2 reshape.175
  90.8 0.7 add_select_fusion.1
  91.5 0.3 scatter-add.20
  91.9 12.6 %rev.18 = bf16[256,2048]{1,0:T(8,128)(2,1)S(1)} reverse(bf16[256,2048]{1,0:T(8,128)(2,1)} %collective-permute-done.2), dimensions={0} | reverse | bytes 2097152 | tf_op jit(solution)/shard_map/rev | solution.py:35
  104.5 0.5 fusion.3
  105.0 0.1 pad_bitcast_fusion.1
  105.1 0.8 copy.44
  106.0 1.2 reshape.178
  107.3 0.7 add_select_fusion
  108.0 0.3 scatter-add.21
  108.3 12.6 %rev.19 = bf16[256,2048]{1,0:T(8,128)(2,1)S(1)} reverse(bf16[256,2048]{1,0:T(8,128)(2,1)} %collective-permute-done.3), dimensions={0} | reverse | bytes 2097152 | tf_op jit(solution)/shard_map/rev | solution.py:35
  120.9 0.5 fusion
  121.4 0.1 pad_bitcast_fusion
  121.5 0.8 copy.45
  122.4 1.2 reshape.181
  123.8 0.3 scatter-add.24
  124.1 0.6 slice_bitcast_fusion
  124.8 107.8 %all-gather.4.cloned.1.call-done = f32[128,2,1024]{2,1,0:T(2,128)} async-done(((f32[1,2,1024]{2,1,0:T(2,128)}), f32[128,2,1024]{2,1,0:T(2,128)}) %all-gather.4.cloned.1.call-update) | async-done | bytes 1048592 | tf_op jit(solution)/shard_map/all_gather | solution.py:43
  232.6 2.2 reduce_sum.59
  (26 shorter events, 1.0 us)
Async XLA Ops:
  6.5 226.0 %all-gather.4.cloned.1.call-start = ((), (), s32[]{:S(2)}) async-start(), calls=%async_computation | async-start | bytes 1056768 | tf_op jit(solution)/shard_map/all_gather | solution.py:43
  8.5 34.4 %copy-start = (bf16[256,2048]{1,0:T(8,128)(2,1)S(1)}, bf16[256,2048]{1,0:T(8,128)(2,1)}, u32[]{:S(2)}) copy-start(bf16[256,2048]{1,0:T(8,128)(2,1)} %param.17) | copy-start | bytes 3145732
  8.5 34.4 %copy-start.1 = (bf16[256,2048]{1,0:T(8,128)(2,1)S(1)}, bf16[256,2048]{1,0:T(8,128)(2,1)}, u32[]{:S(2)}) copy-start(bf16[256,2048]{1,0:T(8,128)(2,1)} %param.14) | copy-start | bytes 3145732
  8.5 18.1 %collective-permute-start = (bf16[256,2048]{1,0:T(8,128)(2,1)S(1)}, bf16[256,2048]{1,0:T(8,128)(2,1)}, u32[]{:S(2)}, u32[]{:S(2)}) collective-permute-start(bf16[256,2048]{1,0:T(8,128)(2,1)S(1)} %multiply_convert_fusion), channel_id=1, source_target_pairs={{0,2},{2,4},{4,6},{6,8},{8,10},{10,12},{12,14},{14,16},{16,18},{18... | collective-permute-start | bytes 3145736 | tf_op jit(solution)/shard_map/ppermute | solution.py:13
  26.6 18.0 %collective-permute-start.1 = (bf16[256,2048]{1,0:T(8,128)(2,1)}, bf16[256,2048]{1,0:T(8,128)(2,1)}, u32[]{:S(2)}, u32[]{:S(2)}) collective-permute-start(bf16[256,2048]{1,0:T(8,128)(2,1)} %collective-permute-done), channel_id=1, source_target_pairs={{0,2},{2,4},{4,6},{6,8},{8,10},{10,12},{12,14},{14,16},{16,18},{18... | collective-permute-start | bytes 3145736 | tf_op jit(solution)/shard_map/ppermute | solution.py:13
  42.9 7.6 %copy-start.4 = (bf16[256,2048]{1,0:T(8,128)(2,1)S(1)}, bf16[256,2048]{1,0:T(8,128)(2,1)}, u32[]{:S(2)}) copy-start(bf16[256,2048]{1,0:T(8,128)(2,1)} %rev.15) | copy-start | bytes 3145732
  43.3 7.2 %copy-start.2 = (bf16[256,2048]{1,0:T(8,128)(2,1)}, bf16[256,2048]{1,0:T(8,128)(2,1)S(1)}, u32[]{:S(2)}) copy-start(bf16[256,2048]{1,0:T(8,128)(2,1)S(1)} %multiply_convert_fusion.1) | copy-start | bytes 3145732
  44.6 41.3 %collective-permute-start.2 = (bf16[256,2048]{1,0:T(8,128)(2,1)}, bf16[256,2048]{1,0:T(8,128)(2,1)}, u32[]{:S(2)}, u32[]{:S(2)}) collective-permute-start(bf16[256,2048]{1,0:T(8,128)(2,1)} %collective-permute-done.1), channel_id=1, source_target_pairs={{0,2},{2,4},{4,6},{6,8},{8,10},{10,12},{12,14},{14,16},{16,18},{18... | collective-permute-start | bytes 3145736 | tf_op jit(solution)/shard_map/ppermute | solution.py:13
  56.7 12.7 %copy-start.3 = (bf16[256,2048]{1,0:T(8,128)(2,1)S(1)}, bf16[256,2048]{1,0:T(8,128)(2,1)}, u32[]{:S(2)}) copy-start(bf16[256,2048]{1,0:T(8,128)(2,1)} %copy-done.2) | copy-start | bytes 3145732
  85.9 22.4 %collective-permute-start.3 = (bf16[256,2048]{1,0:T(8,128)(2,1)}, bf16[256,2048]{1,0:T(8,128)(2,1)}, u32[]{:S(2)}, u32[]{:S(2)}) collective-permute-start(bf16[256,2048]{1,0:T(8,128)(2,1)} %collective-permute-done.2), channel_id=1, source_target_pairs={{0,2},{2,4},{4,6},{6,8},{8,10},{10,12},{12,14},{14,16},{16,18},{18... | collective-permute-start | bytes 3145736 | tf_op jit(solution)/shard_map/ppermute | solution.py:13
Sparse Core Ops, SparseCore 0:
  124.9 107.6 all-gather.3
